TPU v7x, 256 devices: a whole 4x4x8 slice. The times are simulated.
256 devices in a mesh: section: 16 (over x, z_hi), tensor: 16 (over z_lo, y, core).
Axes of the slice: x: 4, y: 4, z: 8 (z_hi: 4, z_lo: 2; z = z_hi * 2 + z_lo), core: 2. Of those that a mesh axis runs over, the one named last changes fastest.
Arguments:
- inputs: bfloat16 [8192, 4096], P('section'), may hold values from -6 to 6
- out_grads: bfloat16 [8192, 11008], P('section', 'tensor'), may hold values from -0.1796875 to 0.1796875
- use_section: int32 [6], replicated, may hold values from 0 to 15, as said below
- a_inverse: float32 [4096, 256], P('section'), may hold values from -0.375 to 0.375
- g_inverse: float32 [11008, 688], P('tensor'), may hold values from -0.21875 to 0.21875
Outputs:
- a_cov: float32 [4096, 4096], P('section', 'tensor')
- g_cov: float32 [11008, 11008], P('section', 'tensor')
- grad: float32 [4096, 11008], P('section', 'tensor')
- precond: float32 [4096, 11008], P('section', 'tensor')
Inputs may be any that keep to these rules, and one draw needn't show every extreme that they name: `use_section`: the entries are distinct copies; the first and the last copy are always among them.
All inputs are finite; a program needn't handle non-finite values.
Results may differ from a plain program's by a relative error of at most 0.015.
Values may be sent and summed in bfloat16 or wider, within the bound.
A program may use at most 128 MiB of HBM per device.

v0:
```python
import jax
import jax.numpy as jnp
from jax import lax
from jax.sharding import PartitionSpec as P

TOK_DEV = 512
USES = 6


def cross(left, right):
    return lax.dot_general(
        left, right, (((0,), (0,)), ((), ())), preferred_element_type=jnp.float32
    )


def on_device(inputs, out_grads, use_section, a_inverse, g_inverse):
    section_here = lax.axis_index("section")
    live = jnp.any(use_section == section_here).astype(jnp.bfloat16)
    inputs_live = inputs * live
    grads_live = out_grads * live
    width_d = inputs.shape[1] // lax.axis_size("tensor")
    column_start = lax.axis_index("tensor") * width_d
    inputs_cols = lax.dynamic_slice_in_dim(inputs_live, column_start, width_d, 1)
    grads_full = lax.all_gather(grads_live, "tensor", axis=1, tiled=True)
    rows_a = inputs_live
    a_sum = lax.psum_scatter(
        cross(rows_a, inputs_cols).astype(jnp.bfloat16), "section", scatter_dimension=0, tiled=True
    ).astype(jnp.float32)
    rows_a = inputs_live
    w_sum = lax.psum_scatter(
        cross(rows_a, grads_live).astype(jnp.bfloat16), "section", scatter_dimension=0, tiled=True
    ).astype(jnp.float32)
    g_cov = lax.psum_scatter(
        cross(grads_full, grads_live).astype(jnp.bfloat16),
        "section",
        scatter_dimension=0,
        tiled=True,
    ).astype(jnp.float32)
    a_cov = a_sum / (USES * TOK_DEV)
    left = jnp.dot(a_inverse, w_sum, precision=lax.Precision.HIGHEST)
    precond = jnp.dot(left, g_inverse, precision=lax.Precision.HIGHEST)
    return (a_cov, g_cov, w_sum, precond)


def solution(mesh):
    return jax.shard_map(
        on_device,
        mesh=mesh,
        in_specs=(
            P("section", None),
            P("section", "tensor"),
            P(),
            P("section", None),
            P("tensor", None),
        ),
        out_specs=(
            P("section", "tensor"),
            P("section", "tensor"),
            P("section", "tensor"),
            P("section", "tensor"),
        ),
        check_vma=False,
    )
```

profile of v0, /device:TPU:1, one launch (start us, length us, event | category | flops | bytes accessed | tf_op | source)
XLA Modules:
  0.0 478.7 jit_solution(11993825967464733299)
XLA Ops:
  8.0 0.0 copy-start
  8.0 0.0 all-gather.2.cloned.1.call-start
  8.1 1.4 compare_reduce_fusion
  10.2 2.0 broadcast_multiply_fusion.1
  12.2 0.0 all-gather.2.cloned.1.call-update
  12.2 0.0 reduce-scatter.4.cloned.1.call-start
  12.2 2.5 broadcast_multiply_fusion
  14.7 0.0 copy-start.1
  14.7 1.9 copy-done.1
  16.7 0.0 copy-start.2
  16.7 2.6 convolution_convert_fusion.2
  19.3 0.0 reduce-scatter.4.cloned.1.call-update
  19.3 0.0 reduce-scatter.8.cloned.1.call-start
  19.4 0.0 copy-done.2
  19.4 7.0 %convolution_convert_fusion.1 = bf16[4096,688]{0,1:T(8,128)(2,1)} fusion(bf16[512,688]{0,1:T(8,128)(2,1)S(1)} %copy-done.2, bf16[512,4096]{1,0:T(8,128)(2,1)} %copy-done.1), kind=kOutput, calls=%fused_computation.1 | convolution fusion | flops 2888499200 | bytes 10534912 | tf_op jit(solution)/shard_map/dot_general | solution.py:11
  26.4 0.0 reduce-scatter.8.cloned.1.call-update
  26.4 0.0 reduce-scatter.6.cloned.1.call-start
  26.5 66.9 %all-gather.2.cloned.1.call-done = bf16[512,11008]{0,1:T(8,128)(2,1)} async-done(((bf16[512,688]{0,1:T(8,128)(2,1)}), bf16[512,11008]{0,1:T(8,128)(2,1)}) %all-gather.2.cloned.1.call-update) | async-done | bytes 11272208 | tf_op jit(solution)/shard_map/all_gather | solution.py:24
  93.3 16.2 %convolution_convert_fusion = bf16[11008,688]{1,0:T(8,128)(2,1)} fusion(bf16[512,11008]{0,1:T(8,128)(2,1)} %all-gather.2.cloned.1.call-done, bf16[512,688]{0,1:T(8,128)(2,1)S(1)} %copy-done.2), kind=kOutput, calls=%fused_computation | convolution fusion | flops 7762841600 | bytes 27123712 | tf_op jit(solution)/shard_map/dot_general | solution.py:11
  109.5 0.0 copy-start.3
  109.5 0.0 reduce-scatter.6.cloned.1.call-update
  109.6 32.7 %reduce-scatter.4.cloned.1.call-done = bf16[256,256]{1,0:T(8,128)(2,1)} async-done(((bf16[4096,256]{1,0:T(8,128)(2,1)}), bf16[256,256]{1,0:T(8,128)(2,1)}) %reduce-scatter.4.cloned.1.call-update) | async-done | bytes 131088 | tf_op jit(solution)/shard_map/reduce_scatter | solution.py:26
  142.3 1.6 convert_multiply_fusion
  143.9 112.7 %reduce-scatter.8.cloned.1.call-done = bf16[256,688]{0,1:T(8,128)(2,1)} async-done(((bf16[4096,688]{0,1:T(8,128)(2,1)}), bf16[256,688]{0,1:T(8,128)(2,1)}) %reduce-scatter.8.cloned.1.call-update) | async-done | bytes 352272 | tf_op jit(solution)/shard_map/reduce_scatter | solution.py:30
  256.6 1.9 convert_element_type.27
  258.5 0.0 copy-done.3
  258.5 1.5 fusion.2
  260.0 0.0 copy-done
  260.0 4.7 fusion.3
  264.7 203.7 %reduce-scatter.6.cloned.1.call-done = bf16[688,688]{1,0:T(8,128)(2,1)} async-done(((bf16[11008,688]{1,0:T(8,128)(2,1)}), bf16[688,688]{1,0:T(8,128)(2,1)}) %reduce-scatter.6.cloned.1.call-update) | async-done | bytes 946704 | tf_op jit(solution)/shard_map/reduce_scatter | solution.py:33
  468.4 2.7 convert_element_type.25
Async XLA Ops:
  8.0 252.0 %copy-start = (f32[688,688]{1,0:T(8,128)S(1)}, f32[688,688]{1,0:T(8,128)}, u32[]{:S(2)}) copy-start(f32[688,688]{1,0:T(8,128)} %param.9) | copy-start | bytes 5680132
  8.0 85.3 %all-gather.2.cloned.1.call-start = ((), (), s32[]{:S(2)}) async-start(), calls=%async_computation.4 | async-start | bytes 11976704 | tf_op jit(solution)/shard_map/all_gather | solution.py:24
  12.2 130.1 %reduce-scatter.4.cloned.1.call-start = ((), (), s32[]{:S(2)}) async-start(), calls=%async_computation.3 | async-start | bytes 2228224 | tf_op jit(solution)/shard_map/reduce_scatter | solution.py:26
  14.7 1.9 copy-start.1
  16.7 2.7 copy-start.2
  19.3 237.3 %reduce-scatter.8.cloned.1.call-start = ((), (), s32[]{:S(2)}) async-start(), calls=%async_computation.6 | async-start | bytes 5988352 | tf_op jit(solution)/shard_map/reduce_scatter | solution.py:30
  26.4 442.0 %reduce-scatter.6.cloned.1.call-start = ((), (), s32[]{:S(2)}) async-start(), calls=%async_computation.5 | async-start | bytes 17965056 | tf_op jit(solution)/shard_map/reduce_scatter | solution.py:33
  109.5 149.0 %copy-start.3 = (f32[256,256]{1,0:T(8,128)S(1)}, f32[256,256]{1,0:T(8,128)}, u32[]{:S(2)}) copy-start(f32[256,256]{1,0:T(8,128)} %param.8) | copy-start | bytes 786436
Sparse Core Ops, SparseCore 0:
  12.3 80.9 all-gather.1
Sparse Core Ops, SparseCore 1:
  19.4 122.8 reduce-scatter.3
  146.4 110.2 reduce-scatter.7
  260.7 207.7 reduce-scatter.5
where the time goes:
time: 479 us
  waiting for transfers between devices  416 us (87%)
  matrix products  32 us (7%)
  between operations  16.4 us (3%)
  other arithmetic  12.1 us (3%)
    reduce_scatter x1, waiting for transfers between devices, on_device(): lax.psum_scatter(cross(grads_full, grads_live).astype(jnp.bfloat16), 'sec...  204 us
    reduce_scatter x1, waiting for transfers between devices, on_device(): lax.psum_scatter(cross(rows_a, grads_live).astype(jnp.bfloat16), 'section...  113 us
    all_gather x1, waiting for transfers between devices, on_device(): grads_full = lax.all_gather(grads_live, 'tensor', axis=1, tiled=True)  66.9 us
    reduce_scatter x1, waiting for transfers between devices, on_device(): lax.psum_scatter(cross(rows_a, inputs_cols).astype(jnp.bfloat16), 'sectio...  32.7 us
    dot_general x3, matrix products, cross(): lax.dot_general(left, right, (((0,), (0,)), ((), ())), preferred_element_...  25.9 us
  transfers between devices with their start and end apart: 4, of which 4 were waited for; matrix products, arithmetic and copies ran while one was open for 8% of the time, Pallas kernels for 0%

commit v1 on v0

v1 whole, which is shorter than its diff:
```python
import jax
import jax.numpy as jnp
from jax import lax
from jax.experimental import pallas as pl
from jax.experimental.pallas import tpu as pltpu
from jax.sharding import PartitionSpec as P

TOK_DEV = 512
USES = 6
N = 16
D = 4096
DB = 256
FB = 688
SUB = 16
PIECE = USES * SUB
HALF = N * PIECE
GA, X, GB = 0, 1, 2
MESH = pl.DeviceIdType.MESH


def cross(left, right):
    return lax.dot_general(
        left, right, (((0,), (0,)), ((), ())), preferred_element_type=jnp.float32
    )


def aligned(value, step):
    return pl.multiple_of(value * step, step)


def kernel(
    inp, grads, use, a_inv, g_inv, a_out, g_out, w_out, p_out,
    rg0, rg1, rx, fg, fx, sg, sx, acc_a, acc_g, acc_w, acc_p, ai, gi, ss, rs, ls,
):
    s, t = lax.axis_index("section"), lax.axis_index("tensor")
    x, z = s // 4, s % 4
    l, y, c = t // 8, (t // 2) % 4, t % 2

    def sec(dx, dz):
        return ((x + dx + 4) % 4) * 4 + (z + dz + 4) % 4

    def ten(dl, dy, dc):
        return (((l + dl) % 2) * 4 + (y + dy + 4) % 4) * 2 + (c + dc) % 2

    bar = pltpu.get_barrier_semaphore()
    for k in range(1, N):
        pl.semaphore_signal(bar, inc=1, device_id=((s + k) % N, t), device_id_type=MESH)
    for d in (ten(1, 0, 0), ten(0, 1, 0), ten(0, -1, 0), ten(0, 0, 1)):
        pl.semaphore_signal(bar, inc=1, device_id=(s, d), device_id_type=MESH)

    @pl.when(s != t)
    def _():
        pl.semaphore_signal(bar, inc=1, device_id=(t, s), device_id_type=MESH)

    loads = [
        pltpu.make_async_copy(a_inv, ai, ls.at[0]),
        pltpu.make_async_copy(g_inv, gi, ls.at[1]),
    ]

    def share(ch, p):
        if ch == X:
            return inp.at[pl.ds(aligned(p, 2 * SUB), 2 * SUB), pl.ds(aligned(t, DB), DB)]
        h = ch // 2
        return grads.at[pl.ds(pl.multiple_of(p * 2 * SUB + h * SUB, SUB), SUB)]

    def slot(ch, k):
        return (rg0, rx, rg1)[ch].at[k]

    own = [pltpu.make_async_copy(share(ch, s), slot(ch, N - 1), ls.at[2 + ch]) for ch in range(3)]
    for cp in loads + own:
        cp.start()
    pl.semaphore_wait(bar, 19 + (s != t).astype(jnp.int32))

    ids = {}

    def sem(key):
        return ids.setdefault(key, len(ids))

    sent = []

    def send(key, src, dst, dev):
        i = sem(key)
        cp = pltpu.make_async_remote_copy(
            src, dst, ss.at[i], rs.at[i], device_id=dev, device_id_type=MESH
        )
        cp.start()
        sent.append(cp)

    def recv(key, ref):
        i = sem(key)
        pltpu.make_async_remote_copy(
            ref, ref, ss.at[i], rs.at[i], device_id=(s, t), device_id_type=MESH
        ).wait_recv()

    def part(bufs, ch, p, half=None):
        g, xx = bufs
        base = p * PIECE
        if ch == X:
            rows = pl.ds(pl.multiple_of(base, PIECE), PIECE)
            return xx.at[:, rows] if half is None else xx.at[half, rows]
        if half is None:
            return g.at[ch // 2, pl.ds(pl.multiple_of(base, PIECE), PIECE)]
        h = PIECE // 2
        return g.at[ch // 2, pl.ds(pl.multiple_of(base + half * h, SUB), h)]

    F, S = (fg, fx), (sg, sx)

    for ch in (GA, X, GB):
        for k in range(1, N):
            p = (s + k) % N
            send(("a", ch, k), share(ch, p), slot(ch, k - 1), (p, t))

    def pick(ch):
        own[ch].wait()
        for k in range(1, N):
            recv(("a", ch, k), slot(ch, k - 1))
        for u in range(USES):
            k = (s - use[u] + 2 * N - 1) % N
            rows = pl.ds(pl.multiple_of(s * PIECE + u * SUB, SUB), SUB)
            if ch == X:
                both = rx[k]
                fx[0, rows, :] = both[:SUB]
                fx[1, rows, :] = both[SUB:]
            else:
                fg[ch // 2, rows, :] = (rg0, rx, rg1)[ch][k]

    def mirror(ch):
        i = sem(("t", ch))
        src, dst = part(F, ch, s), part(S, ch, s)

        @pl.when(s != t)
        def _():
            pltpu.make_async_remote_copy(
                src, dst, ss.at[i], rs.at[i], device_id=(t, s), device_id_type=MESH
            ).start()

        @pl.when(s == t)
        def _():
            pltpu.make_async_copy(src, dst, rs.at[i]).start()

    def mirror_sent(ch):
        i = sem(("t", ch))

        @pl.when(s != t)
        def _():
            ref = part(F, ch, s)
            pltpu.make_async_remote_copy(
                ref, ref, ss.at[i], rs.at[i], device_id=(t, s), device_id_type=MESH
            ).wait_send()

    def along_x(ch, dz):
        p = sec(0, dz)
        for d in (1, -1):
            send(("x", ch, dz, d), part(F, ch, p), part(F, ch, p), (sec(d, 0), t))

    def along_z(ch):
        for d in (1, -1):
            send(("z", ch, d), part(F, ch, s), part(F, ch, s), (sec(0, d), t))

    def z_in(ch):
        for d in (1, -1):
            p = sec(0, -d)
            recv(("z", ch, d), part(F, ch, p))
            r = part(F, ch, p, (1 - d) // 2)
            send(("zf", ch, d), r, r, (sec(0, d), t))
            along_x(ch, -d)

    def z_far(ch):
        for d in (1, -1):
            recv(("zf", ch, d), part(F, ch, sec(0, 2), (1 - d) // 2))
        along_x(ch, 2)

    def x_in(ch, dz):
        for d in (1, -1):
            p = sec(-d, dz)
            recv(("x", ch, dz, d), part(F, ch, p))
            r = part(F, ch, p, (1 - d) // 2)
            send(("xf", ch, dz, d), r, r, (sec(d, 0), t))

    def x_far(ch, dz):
        for d in (1, -1):
            recv(("xf", ch, dz, d), part(F, ch, sec(2, dz), (1 - d) // 2))

    def to_core(ch, dl, dy):
        p = ten(dl, dy, 0)
        send(("c", ch, dl, dy), part(S, ch, p), part(S, ch, p), (s, ten(0, 0, 1)))

    def along_y(ch, dl):
        p = ten(dl, 0, 0)
        for d in (1, -1):
            send(("y", ch, dl, d), part(S, ch, p), part(S, ch, p), (s, ten(0, d, 0)))

    def plane_start(ch):
        recv(("t", ch), part(S, ch, t))
        send(("l", ch), part(S, ch, t), part(S, ch, t), (s, ten(1, 0, 0)))
        along_y(ch, 0)
        to_core(ch, 0, 0)

    def plane_l(ch):
        recv(("l", ch), part(S, ch, ten(1, 0, 0)))
        along_y(ch, 1)
        to_core(ch, 1, 0)

    def plane_y(ch, dl):
        for d in (1, -1):
            p = ten(dl, -d, 0)
            recv(("y", ch, dl, d), part(S, ch, p))
            r = part(S, ch, p, (1 - d) // 2)
            send(("yf", ch, dl, d), r, r, (s, ten(0, d, 0)))
            to_core(ch, dl, -d)

    def plane_far(ch, dl):
        for d in (1, -1):
            recv(("yf", ch, dl, d), part(S, ch, ten(dl, 2, 0), (1 - d) // 2))
        to_core(ch, dl, 2)

    def plane_core(ch):
        for dl in (0, 1):
            for dy in (0, 1, -1, 2):
                recv(("c", ch, dl, dy), part(S, ch, ten(dl, dy, 1)))

    def g_step(h, first):
        step = HALF // 3
        for i in range(3):
            rows = pl.ds(i * step, step)
            prod = cross(sg[h, rows, :], fg[h, rows, :])
            if first and i == 0:
                acc_g[...] = prod
            else:
                acc_g[...] += prod

    def w_step(h):
        prod = cross(sx[h], fg[h])
        if h == 0:
            acc_w[...] = prod
        else:
            acc_w[...] += prod

    pick(GA)
    mirror(GA)
    along_z(GA)
    along_x(GA, 0)
    pick(X)
    mirror(X)
    plane_start(GA)
    z_in(GA)
    pick(GB)
    mirror(GB)
    along_z(GB)
    along_x(GB, 0)
    plane_start(X)
    plane_l(GA)
    x_in(GA, 0)
    z_far(GA)
    plane_y(GA, 0)
    plane_start(GB)
    z_in(GB)
    x_in(GA, -1)
    x_in(GA, 1)
    plane_l(X)
    plane_y(GA, 1)
    plane_far(GA, 0)
    plane_l(GB)
    x_in(GB, 0)
    z_far(GB)
    x_in(GA, 2)
    plane_y(X, 0)
    plane_y(GB, 0)
    plane_far(GA, 1)
    along_z(X)
    along_x(X, 0)
    x_in(GB, -1)
    x_in(GB, 1)
    plane_y(X, 1)
    plane_far(X, 0)
    plane_y(GB, 1)
    plane_far(GB, 0)
    plane_far(X, 1)
    z_in(X)
    x_in(GB, 2)
    plane_far(GB, 1)
    for dz in (0, -1, 1, 2):
        x_far(GA, dz)
    plane_core(GA)
    g_step(0, True)
    x_in(X, 0)
    z_far(X)
    plane_core(X)
    w_step(0)
    x_in(X, -1)
    x_in(X, 1)
    for dz in (0, -1, 1, 2):
        x_far(GB, dz)
    plane_core(GB)
    w_step(1)
    x_in(X, 2)
    outs = [pltpu.make_async_copy(acc_w, w_out, ls.at[5])]
    outs[-1].start()
    g_step(1, False)
    outs.append(pltpu.make_async_copy(acc_g, g_out, ls.at[6]))
    outs[-1].start()
    for cp in loads:
        cp.wait()
    left = jnp.dot(
        ai[...], acc_w[...], precision=lax.Precision.HIGHEST, preferred_element_type=jnp.float32
    )
    acc_p[...] = jnp.dot(
        left, gi[...], precision=lax.Precision.HIGHEST, preferred_element_type=jnp.float32
    )
    outs.append(pltpu.make_async_copy(acc_p, p_out, ls.at[7]))
    outs[-1].start()
    for dz in (0, -1, 1, 2):
        x_far(X, dz)
    acc_a[...] = (cross(sx[0], fx[0]) + cross(sx[1], fx[1])) / (USES * TOK_DEV)
    outs.append(pltpu.make_async_copy(acc_a, a_out, ls.at[8]))
    outs[-1].start()
    for cp in sent:
        cp.wait_send()
    for ch in range(3):
        mirror_sent(ch)
    for cp in outs:
        cp.wait()
    assert len(ids) <= 192, len(ids)


def on_device(inputs, out_grads, use_section, a_inverse, g_inverse):
    bf, f32 = jnp.bfloat16, jnp.float32
    any_space = pl.BlockSpec(memory_space=pl.ANY)
    return pl.pallas_call(
        kernel,
        out_shape=(
            jax.ShapeDtypeStruct((DB, DB), f32),
            jax.ShapeDtypeStruct((FB, FB), f32),
            jax.ShapeDtypeStruct((DB, FB), f32),
            jax.ShapeDtypeStruct((DB, FB), f32),
        ),
        in_specs=[
            any_space,
            any_space,
            pl.BlockSpec(memory_space=pltpu.SMEM),
            any_space,
            any_space,
        ],
        out_specs=(any_space,) * 4,
        scratch_shapes=[
            pltpu.VMEM((N, SUB, FB), bf),
            pltpu.VMEM((N, SUB, FB), bf),
            pltpu.VMEM((N, 2 * SUB, DB), bf),
            pltpu.VMEM((2, HALF, FB), bf),
            pltpu.VMEM((2, HALF, DB), bf),
            pltpu.VMEM((2, HALF, FB), bf),
            pltpu.VMEM((2, HALF, DB), bf),
            pltpu.VMEM((DB, DB), f32),
            pltpu.VMEM((FB, FB), f32),
            pltpu.VMEM((DB, FB), f32),
            pltpu.VMEM((DB, FB), f32),
            pltpu.VMEM((DB, DB), f32),
            pltpu.VMEM((FB, FB), f32),
            pltpu.SemaphoreType.DMA((192,)),
            pltpu.SemaphoreType.DMA((192,)),
            pltpu.SemaphoreType.DMA((9,)),
        ],
        compiler_params=pltpu.CompilerParams(
            collective_id=0, has_side_effects=True, vmem_limit_bytes=48 * 2**20
        ),
        name="kfac",
    )(inputs, out_grads, use_section, a_inverse, g_inverse)


def solution(mesh):
    return jax.shard_map(
        on_device,
        mesh=mesh,
        in_specs=(
            P("section", None),
            P("section", "tensor"),
            P(),
            P("section", None),
            P("tensor", None),
        ),
        out_specs=(
            P("section", "tensor"),
            P("section", "tensor"),
            P("section", "tensor"),
            P("section", "tensor"),
        ),
        check_vma=False,
    )
```

time: 479 us -> 140 us (0.29)
  the two profiles are of different devices: /device:TPU:1 before, /device:TPU:22 now
where the time goes in v1:
time: 140 us; the launch traced here: 139 us
  Pallas kernels  127 us (91%)
  local copies, waits for them, and re-layouts  11.2 us (8%)
    pallas_call x1, Pallas kernels, on_device(): pl.pallas_call(kernel, out_shape=(jax.ShapeDtypeStruct((DB, DB), f32), ja...  127 us
    unnamed x11, local copies, waits for them, and re-layouts  6.76 us
    pallas_call x2, local copies, waits for them, and re-layouts, on_device(): pl.pallas_call(kernel, out_shape=(jax.ShapeDtypeStruct((DB, DB), f32), ja...  4.47 us

profile of v1, /device:TPU:22, one launch (start us, length us, event | category | flops | bytes accessed | tf_op | source)
XLA Modules:
  0.0 139.3 jit_solution(4620080105283359216)
XLA Ops:
  0.6 1.4 copy.9.grads
  2.0 0.0 copy-start.2
  2.0 0.9 copy-done.2
  3.0 0.0 copy-start.3
  3.0 0.7 copy-done.3
  3.6 127.4 %kfac.1 = (f32[256,256]{1,0:T(8,128)S(1)}, f32[688,688]{1,0:T(8,128)S(1)}, f32[256,688]{1,0:T(8,128)S(1)}, f32[256,688]{1,0:T(8,128)S(1)}) custom-call(bf16[512,4096]{1,0:T(8,128)(2,1)} %inp.1, bf16[512,688]{1,0:T(8,128)(2,1)S(1)} %copy.9.grads, s32[6]{0:T(128)S(1)} %copy-done.3, f32[256,256]{1,0:T(8,128)S(1)} %copy-done.2, f32[688,688]{1,0:T(8,128)} %g_inv.1), custom_call_target="tpu_custom_call" | custom-call | tf_op jit(solution)/shard_map/kfac/pallas_call | solution.py:329
  131.1 0.0 copy-start
  131.1 0.9 copy-done
  132.0 0.0 copy-start.1
  132.0 0.9 copy-done.1
  132.8 2.2 %copy.10 = f32[256,688]{0,1:T(8,128)} copy(f32[256,688]{1,0:T(8,128)} %copy-done.1) | data formatting | bytes 1409024 | tf_op jit(solution)/shard_map/kfac/pallas_call | solution.py:329
  135.1 2.2 %copy.11 = f32[256,688]{0,1:T(8,128)} copy(f32[256,688]{1,0:T(8,128)} %copy-done) | data formatting | bytes 1409024 | tf_op jit(solution)/shard_map/kfac/pallas_call | solution.py:329
  137.3 0.7 copy.14
  138.0 1.3 copy.15
Async XLA Ops:
  2.0 1.0 copy-start.2
  3.0 0.7 copy-start.3
  131.1 0.9 copy-start
  132.0 0.9 copy-start.1

commit v2 on v1

v2 whole, which is shorter than its diff:
```python
import jax
import jax.numpy as jnp
from jax import lax
from jax.experimental import pallas as pl
from jax.experimental.pallas import tpu as pltpu
from jax.sharding import PartitionSpec as P

TOK_DEV = 512
USES = 6
N = 16
D = 4096
DB = 256
FB = 688
SUB = 16
PIECE = USES * SUB
HALF = N * PIECE
GA, X, GB = 0, 1, 2
DX = (0, 1, -1, 2)
MESH = pl.DeviceIdType.MESH


def cross(left, right):
    return lax.dot_general(
        left, right, (((0,), (0,)), ((), ())), preferred_element_type=jnp.float32
    )


def halves(value):
    high = value.astype(jnp.bfloat16)
    return high, (value - high.astype(jnp.float32)).astype(jnp.bfloat16)


def exact(left, right, i, j):
    def dot(p, q):
        return lax.dot_general(
            p, q, (((i,), (j,)), ((), ())), preferred_element_type=jnp.float32
        )

    (lh, ll), (rh, rl) = halves(left), halves(right)
    return dot(lh, rh) + (dot(lh, rl) + dot(ll, rh))


def aligned(value, step):
    return pl.multiple_of(value * step, step)


def kernel(
    inp, grads, use, a_inv, g_inv, a_out, g_out, w_out, p_out,
    rg0, rg1, rx, mg, mx, fg, fx, sg, sx, acc_a, acc_g, acc_w, acc_p, ai, gi, ss, rs, ls,
):
    s, t = lax.axis_index("section"), lax.axis_index("tensor")
    x, z = s // 4, s % 4
    l, y, c = t // 8, (t // 2) % 4, t % 2

    def sec(dx, dz):
        return ((x + dx + 8) % 4) * 4 + (z + dz + 8) % 4

    def ten(dl, dy, dc):
        return (((l + dl) % 2) * 4 + (y + dy + 4) % 4) * 2 + (c + dc) % 2

    bar = pltpu.get_barrier_semaphore()
    for k in range(1, N):
        pl.semaphore_signal(bar, inc=1, device_id=((s + k) % N, t), device_id_type=MESH)
    for d in (ten(1, 0, 0), ten(0, 1, 0), ten(0, -1, 0), ten(0, 0, 1)):
        pl.semaphore_signal(bar, inc=1, device_id=(s, d), device_id_type=MESH)

    def place(a, b, d):
        return l * 8 + a * 4 + b * 2 + d

    x0, z1, z0 = x % 2, z // 2, z % 2
    swap = place((y // 2 + x0) % 2, (c + z0) % 2, (y % 2 + z1) % 2)
    back = place((y // 2 + x0) % 2, (c + z1) % 2, (y % 2 + z0) % 2)

    @pl.when(swap != t)
    def _():
        pl.semaphore_signal(bar, inc=1, device_id=(s, back), device_id_type=MESH)

    loads = [
        pltpu.make_async_copy(a_inv, ai, ls.at[0]),
        pltpu.make_async_copy(g_inv, gi, ls.at[1]),
    ]

    def share(ch, p):
        if ch == X:
            return inp.at[pl.ds(aligned(p, 2 * SUB), 2 * SUB), pl.ds(aligned(t, DB), DB)]
        h = ch // 2
        return grads.at[pl.ds(pl.multiple_of(p * 2 * SUB + h * SUB, SUB), SUB)]

    def slot(ch, k):
        return (rg0, rx, rg1)[ch].at[k]

    own = [pltpu.make_async_copy(share(ch, s), slot(ch, N - 1), ls.at[2 + ch]) for ch in range(3)]
    for cp in loads + own:
        cp.start()
    pl.semaphore_wait(bar, 19 + (swap != t).astype(jnp.int32))

    ids = {}

    def sem(key):
        return ids.setdefault(key, len(ids))

    sent = []
    late = []

    def send(key, src, dst, dev):
        i = sem(key)
        cp = pltpu.make_async_remote_copy(
            src, dst, ss.at[i], rs.at[i], device_id=dev, device_id_type=MESH
        )
        cp.start()
        sent.append(cp)

    def recv(key, ref):
        recv_at(sem(key), ref)

    def recv_at(i, ref):
        pltpu.make_async_remote_copy(
            ref, ref, ss.at[i], rs.at[i], device_id=(s, t), device_id_type=MESH
        ).wait_recv()

    def part(bufs, ch, p, half=None):
        g, xx = bufs
        base = p * PIECE
        if ch == X:
            rows = pl.ds(pl.multiple_of(base, PIECE), PIECE)
            return xx.at[:, rows] if half is None else xx.at[half, rows]
        if half is None:
            return g.at[ch // 2, pl.ds(pl.multiple_of(base, PIECE), PIECE)]
        h = PIECE // 2
        return g.at[ch // 2, pl.ds(pl.multiple_of(base + half * h, SUB), h)]

    F, S = (fg, fx), (sg, sx)

    def deal(ch):
        for k in range(1, N):
            p = (s + k) % N
            send(("a", ch, k), share(ch, p), slot(ch, k - 1), (p, t))

    def pick(ch):
        own[ch].wait()
        for k in range(1, N):
            recv(("a", ch, k), slot(ch, k - 1))
        for u in range(USES):
            k = (s - use[u] + 2 * N - 1) % N
            rows = pl.ds(pl.multiple_of(s * PIECE + u * SUB, SUB), SUB)
            if ch == X:
                both = rx[k]
                fx[0, rows, :] = both[:SUB]
                fx[1, rows, :] = both[SUB:]
            else:
                fg[ch // 2, rows, :] = (rg0, rx, rg1)[ch][k]

    def along_x(ch, dz):
        p = sec(0, dz)
        for d in (1, -1):
            send(("x", ch, dz, d), part(F, ch, p), part(F, ch, p), (sec(d, 0), t))

    def along_z(ch):
        for d in (1, -1):
            send(("z", ch, d), part(F, ch, s), part(F, ch, s), (sec(0, d), t))

    def z_in(ch):
        i = sem(("zf", ch))
        for d in (1, -1):
            p = sec(0, -d)
            ref = part(F, ch, p)
            recv(("z", ch, d), ref)

            @pl.when(x // 2 == (1 + d) // 2)
            def _():
                pltpu.make_async_remote_copy(
                    ref, ref, ss.at[i], rs.at[i], device_id=(sec(0, d), t), device_id_type=MESH
                ).start()

            along_x(ch, -d)

        def sent_all():
            ref = part(F, ch, s)
            pltpu.make_async_copy(ref, ref, ss.at[i]).wait()

        late.append(sent_all)

    def z_far(ch):
        recv(("zf", ch), part(F, ch, sec(0, 2)))
        along_x(ch, 2)

    def x_in(ch, dz):
        for d in (1, -1):
            p = sec(-d, dz)
            recv(("x", ch, dz, d), part(F, ch, p))
            r = part(F, ch, p, (1 - d) // 2)
            send(("xf", ch, dz, d), r, r, (sec(d, 0), t))

    def x_far(ch, dz):
        for d in (1, -1):
            recv(("xf", ch, dz, d), part(F, ch, sec(2, dz), (1 - d) // 2))

    ring = l == s // 8

    def mid(ch):
        return mx if ch == X else mg.at[ch // 2]

    def guarded(out, i, here, src, dst, dev):
        @pl.when(jnp.logical_not(here))
        def _():
            pltpu.make_async_remote_copy(
                src, dst, ss.at[out], rs.at[i], device_id=dev, device_id_type=MESH
            ).start()

        @pl.when(here)
        def _():
            pltpu.make_async_copy(src, dst, rs.at[i]).start()

        def sent_all():
            @pl.when(jnp.logical_not(here))
            def _():
                pltpu.make_async_copy(src, src, ss.at[out]).wait()

        late.append(sent_all)

    def turn_y(ch):
        i = sem(("t1", ch))
        guarded(i, i, swap == t, part(F, ch, s), mid(ch), (s, swap))

    def turn_s(ch):
        recv(("t1", ch), mid(ch))
        to = back
        i = sem(("t2", ch, 0))
        assert sem(("t2", ch, 1)) == i + 1
        guarded(i, i + s // 8, s == to, mid(ch), part(S, ch, s), (to, t))

    def mine(dy, dc, e):
        yy, cc = (y + dy + 4) % 4, (c + dc) % 2
        return 8 * e + (yy // 2 + x0) % 2 * 4 + (cc + z1) % 2 * 2 + (yy % 2 + z0) % 2

    def push(key, ch, p, dev, half=None):
        ref = part(S, ch, p, half)
        send(key, ref, ref, dev)

    def over_l(ch, e):
        p = mine(0, 0, e)
        ref = part(S, ch, p)
        i = sem(("l", ch, e))

        @pl.when(ring)
        def _():
            recv(("t2", ch, e), ref)
            pltpu.make_async_remote_copy(
                ref, ref, ss.at[i], rs.at[i], device_id=(s, ten(1, 0, 0)), device_id_type=MESH
            ).start()

        def sent_all():
            @pl.when(ring)
            def _():
                pltpu.make_async_copy(ref, ref, ss.at[i]).wait()

        late.append(sent_all)

    def start(ch, e):
        p = mine(0, 0, e)

        @pl.when(jnp.logical_not(ring))
        def _():
            recv(("l", ch, e), part(S, ch, p))

        for d in (1, -1):
            push(("y", ch, e, d), ch, p, (s, ten(0, d, 0)))
        push(("c", ch, e, 0), ch, p, (s, ten(0, 0, 1)))

    def y_in(ch, e):
        for d in (1, -1):
            p = mine(-d, 0, e)
            recv(("y", ch, e, d), part(S, ch, p))
            push(("yf", ch, e, d), ch, p, (s, ten(0, d, 0)), (1 - d) // 2)
            push(("c", ch, e, -d), ch, p, (s, ten(0, 0, 1)))

    def y_far(ch, e):
        p = mine(2, 0, e)
        for d in (1, -1):
            recv(("yf", ch, e, d), part(S, ch, p, (1 - d) // 2))
        push(("c", ch, e, 2), ch, p, (s, ten(0, 0, 1)))

    def c_in(ch):
        for e in (0, 1):
            for dy in DX:
                recv(("c", ch, e, dy), part(S, ch, mine(dy, 1, e)))

    def g_step(h, dx):
        rows = pl.ds(pl.multiple_of(sec(dx, -z) * PIECE, 4 * PIECE), 4 * PIECE)
        prod = cross(sg[h, rows, :], fg[h, rows, :])
        if h == 0 and dx == 0:
            acc_g[...] = prod
        else:
            acc_g[...] += prod

    def w_step(h, dx):
        rows = pl.ds(pl.multiple_of(sec(dx, -z) * PIECE, 4 * PIECE), 4 * PIECE)
        prod = cross(fg[h, rows, :], sx[h, rows, :])
        if h == 0 and dx == 0:
            acc_w[...] = prod
        else:
            acc_w[...] += prod

    deal(GA)
    deal(X)
    deal(GB)
    pick(GA)
    turn_y(GA)
    along_x(GA, 0)
    turn_s(GA)
    along_z(GA)
    pick(X)
    turn_y(X)
    along_x(X, 0)
    turn_s(X)
    pick(GB)
    turn_y(GB)
    along_x(GB, 0)
    turn_s(GB)
    along_z(GB)
    z_in(GA)
    x_in(GA, 0)
    over_l(GA, 0)
    over_l(GA, 1)
    over_l(X, 0)
    over_l(X, 1)
    x_in(GB, 0)
    start(GA, 0)
    start(GA, 1)
    z_in(GB)
    along_z(X)
    z_far(GA)
    over_l(GB, 0)
    over_l(GB, 1)
    start(X, 0)
    start(X, 1)
    x_far(GA, 0)
    x_in(GA, -1)
    x_in(GA, 1)
    y_in(GA, 0)
    y_in(GA, 1)
    z_far(GB)
    start(GB, 0)
    start(GB, 1)
    x_in(GA, 2)
    x_far(GB, 0)
    z_in(X)
    x_far(GA, -1)
    x_far(GA, 1)
    x_in(X, 0)
    y_in(X, 0)
    y_in(X, 1)
    y_far(GA, 0)
    y_far(GA, 1)
    x_in(GB, -1)
    x_in(GB, 1)
    z_far(X)
    y_in(GB, 0)
    y_in(GB, 1)
    y_far(X, 0)
    y_far(X, 1)
    x_in(GB, 2)
    x_far(GA, 2)
    x_in(X, -1)
    x_in(X, 1)
    y_far(GB, 0)
    y_far(GB, 1)
    c_in(GA)
    g_step(0, 0)
    x_far(GB, -1)
    x_far(GB, 1)
    x_in(X, 2)
    g_step(0, 1)
    g_step(0, -1)
    g_step(0, 2)
    c_in(X)
    w_step(0, 0)
    w_step(0, 1)
    w_step(0, -1)
    w_step(0, 2)
    w_step(1, 0)
    w_step(1, 1)
    w_step(1, -1)
    c_in(GB)
    g_step(1, 0)
    g_step(1, 1)
    g_step(1, -1)
    x_far(GB, 2)
    w_step(1, 2)
    outs = [pltpu.make_async_copy(acc_w, w_out, ls.at[5])]
    outs[-1].start()
    g_step(1, 2)
    outs.append(pltpu.make_async_copy(acc_g, g_out, ls.at[6]))
    outs[-1].start()
    for cp in loads:
        cp.wait()
    left = exact(acc_w[...], ai[...], 1, 1)
    acc_p[...] = exact(gi[...], left, 0, 0)
    outs.append(pltpu.make_async_copy(acc_p, p_out, ls.at[7]))
    outs[-1].start()
    for dz in DX:
        x_far(X, dz)
    acc_a[...] = (cross(sx[0], fx[0]) + cross(sx[1], fx[1])) / (USES * TOK_DEV)
    outs.append(pltpu.make_async_copy(acc_a, a_out, ls.at[8]))
    outs[-1].start()
    for cp in sent:
        cp.wait_send()
    for wait in late:
        wait()

    for cp in outs:
        cp.wait()
    assert len(ids) <= 256, len(ids)


def on_device(inputs, out_grads, use_section, a_inverse, g_inverse):
    bf, f32 = jnp.bfloat16, jnp.float32
    hbm = pl.BlockSpec(memory_space=pltpu.HBM)
    a_cov, g_cov, grad, precond = pl.pallas_call(
        kernel,
        out_shape=(
            jax.ShapeDtypeStruct((DB, DB), f32),
            jax.ShapeDtypeStruct((FB, FB), f32),
            jax.ShapeDtypeStruct((FB, DB), f32),
            jax.ShapeDtypeStruct((FB, DB), f32),
        ),
        in_specs=[
            hbm,
            hbm,
            pl.BlockSpec(memory_space=pltpu.SMEM),
            hbm,
            hbm,
        ],
        out_specs=(hbm,) * 4,
        scratch_shapes=[
            pltpu.VMEM((N, SUB, FB), bf),
            pltpu.VMEM((N, SUB, FB), bf),
            pltpu.VMEM((N, 2 * SUB, DB), bf),
            pltpu.VMEM((2, PIECE, FB), bf),
            pltpu.VMEM((2, PIECE, DB), bf),
            pltpu.VMEM((2, HALF, FB), bf),
            pltpu.VMEM((2, HALF, DB), bf),
            pltpu.VMEM((2, HALF, FB), bf),
            pltpu.VMEM((2, HALF, DB), bf),
            pltpu.VMEM((DB, DB), f32),
            pltpu.VMEM((FB, FB), f32),
            pltpu.VMEM((FB, DB), f32),
            pltpu.VMEM((FB, DB), f32),
            pltpu.VMEM((DB, DB), f32),
            pltpu.VMEM((FB, FB), f32),
            pltpu.SemaphoreType.DMA((256,)),
            pltpu.SemaphoreType.DMA((256,)),
            pltpu.SemaphoreType.DMA((9,)),
        ],
        compiler_params=pltpu.CompilerParams(
            collective_id=0, has_side_effects=True, vmem_limit_bytes=48 * 2**20
        ),
        name="kfac",
    )(inputs, out_grads, use_section, a_inverse, g_inverse)
    return a_cov, g_cov, grad.T, precond.T


def solution(mesh):
    return jax.shard_map(
        on_device,
        mesh=mesh,
        in_specs=(
            P("section", None),
            P("section", "tensor"),
            P(),
            P("section", None),
            P("tensor", None),
        ),
        out_specs=(
            P("section", "tensor"),
            P("section", "tensor"),
            P("section", "tensor"),
            P("section", "tensor"),
        ),
        check_vma=False,
    )
```

time: 140 us -> 121 us (0.86)
  the two profiles are of different devices: /device:TPU:22 before, /device:TPU:1 now
where the time goes in v2:
time: 121 us; the launch traced here: 119 us
  Pallas kernels  112 us (93%)
  local copies, waits for them, and re-layouts  6.71 us (6%)
    pallas_call x1, Pallas kernels, on_device(): pl.pallas_call(kernel, out_shape=(jax.ShapeDtypeStruct((DB, DB), f32), ja...  112 us
    unnamed x9, local copies, waits for them, and re-layouts  6.71 us

profile of v2, /device:TPU:1, one launch (start us, length us, event | category | flops | bytes accessed | tf_op | source)
XLA Modules:
  0.0 119.3 jit_solution(4190706076976697077)
XLA Ops:
  0.6 1.4 %copy.9.grads = bf16[512,688]{1,0:T(8,128)(2,1)S(1)} copy(bf16[512,688]{0,1:T(8,128)(2,1)} %param.6) | data formatting | bytes 1409024 | tf_op args[1]
  2.0 0.0 copy-start
  2.0 0.9 copy-done
  3.0 0.0 copy-start.1
  3.0 0.7 copy-done.1
  3.6 111.9 %kfac.1 = (f32[256,256]{1,0:T(8,128)S(1)}, f32[688,688]{1,0:T(8,128)S(1)}, f32[688,256]{1,0:T(8,128)S(1)}, f32[688,256]{1,0:T(8,128)S(1)}) custom-call(bf16[512,4096]{1,0:T(8,128)(2,1)} %inp.1, bf16[512,688]{1,0:T(8,128)(2,1)S(1)} %copy.9.grads, s32[6]{0:T(128)S(1)} %copy-done.1, f32[256,256]{1,0:T(8,128)S(1)} %copy-done, f32[688,688]{1,0:T(8,128)} %g_inv.1), custom_call_target="tpu_custom_call" | custom-call | tf_op jit(solution)/shard_map/kfac/pallas_call | solution.py:419
  115.6 0.7 copy.14
  116.3 1.3 %copy.15 = f32[688,688]{1,0:T(8,128)} copy(f32[688,688]{1,0:T(8,128)S(1)} %get-tuple-element.17) | data formatting | bytes 3786752
  117.6 0.9 copy.16
  118.4 0.9 copy.17
Async XLA Ops:
  2.0 1.0 copy-start
  3.0 0.7 copy-start.1

commit v3 on v2

--- a/solution.py
+++ b/solution.py
@@ -288,10 +288,27 @@
     def g_step(h, dx):
         rows = pl.ds(pl.multiple_of(sec(dx, -z) * PIECE, 4 * PIECE), 4 * PIECE)
         prod = cross(sg[h, rows, :], fg[h, rows, :])
-        if h == 0 and dx == 0:
+        if dx == 0 and h == 0:
             acc_g[...] = prod
         else:
             acc_g[...] += prod
+
+    def g_half(h):
+        step = HALF
+        for i in range(1):
+            rows = pl.ds(i * step, step)
+            prod = cross(sg[h, rows, :], fg[h, rows, :])
+            if h == 0 and i == 0:
+                acc_g[...] = prod
+            else:
+                acc_g[...] += prod
+
+    def w_half(h):
+        prod = cross(fg[h], sx[h])
+        if h == 0:
+            acc_w[...] = prod
+        else:
+            acc_w[...] += prod
 
     def w_step(h, dx):
         rows = pl.ds(pl.multiple_of(sec(dx, -z) * PIECE, 4 * PIECE), 4 * PIECE)
@@ -307,8 +324,8 @@
     pick(GA)
     turn_y(GA)
     along_x(GA, 0)
+    along_z(GA)
     turn_s(GA)
-    along_z(GA)
     pick(X)
     turn_y(X)
     along_x(X, 0)
@@ -316,8 +333,8 @@
     pick(GB)
     turn_y(GB)
     along_x(GB, 0)
+    along_z(GB)
     turn_s(GB)
-    along_z(GB)
     z_in(GA)
     x_in(GA, 0)
     over_l(GA, 0)
@@ -361,42 +378,33 @@
     y_far(X, 1)
     x_in(GB, 2)
     x_far(GA, 2)
+    c_in(GA)
+    g_half(0)
     x_in(X, -1)
     x_in(X, 1)
+    c_in(X)
+    w_half(0)
     y_far(GB, 0)
     y_far(GB, 1)
-    c_in(GA)
-    g_step(0, 0)
+    w_step(1, 0)
     x_far(GB, -1)
+    w_step(1, 1)
     x_far(GB, 1)
+    w_step(1, -1)
     x_in(X, 2)
-    g_step(0, 1)
-    g_step(0, -1)
-    g_step(0, 2)
-    c_in(X)
-    w_step(0, 0)
-    w_step(0, 1)
-    w_step(0, -1)
-    w_step(0, 2)
-    w_step(1, 0)
-    w_step(1, 1)
-    w_step(1, -1)
-    c_in(GB)
-    g_step(1, 0)
-    g_step(1, 1)
-    g_step(1, -1)
     x_far(GB, 2)
     w_step(1, 2)
     outs = [pltpu.make_async_copy(acc_w, w_out, ls.at[5])]
-    outs[-1].start()
-    g_step(1, 2)
-    outs.append(pltpu.make_async_copy(acc_g, g_out, ls.at[6]))
     outs[-1].start()
     for cp in loads:
         cp.wait()
     left = exact(acc_w[...], ai[...], 1, 1)
     acc_p[...] = exact(gi[...], left, 0, 0)
     outs.append(pltpu.make_async_copy(acc_p, p_out, ls.at[7]))
+    outs[-1].start()
+    c_in(GB)
+    g_half(1)
+    outs.append(pltpu.make_async_copy(acc_g, g_out, ls.at[6]))
     outs[-1].start()
     for dz in DX:
         x_far(X, dz)
@@ -411,6 +419,17 @@
     for cp in outs:
         cp.wait()
     assert len(ids) <= 256, len(ids)
+
+
+def store(*refs):
+    sources, results, sems = refs[:4], refs[4:8], refs[8]
+    copies = [
+        pltpu.make_async_copy(a, b, sems.at[i]) for i, (a, b) in enumerate(zip(sources, results))
+    ]
+    for cp in copies:
+        cp.start()
+    for cp in copies:
+        cp.wait()
 
 
 def on_device(inputs, out_grads, use_section, a_inverse, g_inverse):
@@ -457,6 +476,16 @@
         ),
         name="kfac",
     )(inputs, out_grads, use_section, a_inverse, g_inverse)
+    results = (a_cov, g_cov, grad, precond)
+    a_cov, g_cov, grad, precond = pl.pallas_call(
+        store,
+        out_shape=tuple(jax.ShapeDtypeStruct(v.shape, f32) for v in results),
+        in_specs=[pl.BlockSpec(memory_space=pl.ANY)] * 4,
+        out_specs=(pl.BlockSpec(memory_space=pl.ANY),) * 4,
+        scratch_shapes=[pltpu.SemaphoreType.DMA((4,))],
+        compiler_params=pltpu.CompilerParams(vmem_limit_bytes=2**20),
+        name="store",
+    )(*results)
     return a_cov, g_cov, grad.T, precond.T
 
 

time: 121 us -> 111 us (0.917); the launches traced: 119 us -> 111 us
  Pallas kernels: 112 us -> 108 us
  local copies, waits for them, and re-layouts: 6.71 us -> 2.98 us
    pallas_call x1, Pallas kernels: 112 us -> 106 us  [on_device(): pl.pallas_call(kernel, out_shape=(jax.ShapeDtypeStruct((DB, DB), f32), ja...]
    unnamed x9 -> x5, local copies, waits for them, and re-layouts: 6.71 us -> 2.98 us
    pallas_call x0 -> x1, Pallas kernels: none -> 1.9 us  [on_device(): pl.pallas_call(store, out_shape=tuple((jax.ShapeDtypeStruct(v.shape, f32)...]
where the time goes in v3:
time: 111 us
  Pallas kernels  108 us (97%)
  local copies, waits for them, and re-layouts  2.98 us (3%)
    pallas_call x1, Pallas kernels, on_device(): pl.pallas_call(kernel, out_shape=(jax.ShapeDtypeStruct((DB, DB), f32), ja...  106 us
    unnamed x5, local copies, waits for them, and re-layouts  2.98 us

profile of v3, /device:TPU:1, one launch (start us, length us, event | category | flops | bytes accessed | tf_op | source)
XLA Modules:
  0.0 111.3 jit_solution(3547803487997642660)
XLA Ops:
  0.6 1.4 %copy.9.grads = bf16[512,688]{1,0:T(8,128)(2,1)S(1)} copy(bf16[512,688]{0,1:T(8,128)(2,1)} %param.6) | data formatting | bytes 1409024 | tf_op args[1]
  2.0 0.0 copy-start
  2.0 0.9 copy-done
  3.0 0.0 copy-start.1
  3.0 0.7 copy-done.1
  3.6 105.8 %kfac.1 = (f32[256,256]{1,0:T(8,128)S(1)}, f32[688,688]{1,0:T(8,128)S(1)}, f32[688,256]{1,0:T(8,128)S(1)}, f32[688,256]{1,0:T(8,128)S(1)}) custom-call(bf16[512,4096]{1,0:T(8,128)(2,1)} %inp.1, bf16[512,688]{1,0:T(8,128)(2,1)S(1)} %copy.9.grads, s32[6]{0:T(128)S(1)} %copy-done.1, f32[256,256]{1,0:T(8,128)S(1)} %copy-done, f32[688,688]{1,0:T(8,128)} %g_inv.1), custom_call_target="tpu_custom_call" | custom-call | tf_op jit(solution)/shard_map/kfac/pallas_call | solution.py:438
  109.4 1.9 %store.1 = (f32[256,256]{1,0:T(8,128)}, f32[688,688]{1,0:T(8,128)}, f32[688,256]{1,0:T(8,128)}, f32[688,256]{1,0:T(8,128)}) custom-call(f32[256,256]{1,0:T(8,128)S(1)} %get-tuple-element.12.refs_0_, f32[688,688]{1,0:T(8,128)S(1)} %get-tuple-element.13.refs_1_, f32[688,256]{1,0:T(8,128)S(1)} %get-tuple-element.14.refs_2_, ...), custom_call_target="tpu_custom_call" | custom-call | tf_op jit(solution)/shard_map/store/pallas_call | solution.py:480
Async XLA Ops:
  2.0 1.0 copy-start
  3.0 0.7 copy-start.1

commit v4 on v3

--- a/solution.py
+++ b/solution.py
@@ -342,13 +342,13 @@
     over_l(X, 0)
     over_l(X, 1)
     x_in(GB, 0)
+    z_in(GB)
     start(GA, 0)
     start(GA, 1)
-    z_in(GB)
-    along_z(X)
     z_far(GA)
     over_l(GB, 0)
     over_l(GB, 1)
+    along_z(X)
     start(X, 0)
     start(X, 1)
     x_far(GA, 0)
@@ -391,7 +391,10 @@
     w_step(1, 1)
     x_far(GB, 1)
     w_step(1, -1)
+    c_in(GB)
+    g_step(1, 0)
     x_in(X, 2)
+    g_step(1, 1)
     x_far(GB, 2)
     w_step(1, 2)
     outs = [pltpu.make_async_copy(acc_w, w_out, ls.at[5])]
@@ -402,8 +405,8 @@
     acc_p[...] = exact(gi[...], left, 0, 0)
     outs.append(pltpu.make_async_copy(acc_p, p_out, ls.at[7]))
     outs[-1].start()
-    c_in(GB)
-    g_half(1)
+    g_step(1, -1)
+    g_step(1, 2)
     outs.append(pltpu.make_async_copy(acc_g, g_out, ls.at[6]))
     outs[-1].start()
     for dz in DX:

time: 111 us -> 112 us (level); the launches traced: 111 us -> 111 us
  no operation moved by 1% of the time
where the time goes in v4:
time: 112 us; the launch traced here: 111 us
  Pallas kernels  107 us (96%)
  local copies, waits for them, and re-layouts  2.98 us (3%)
    pallas_call x1, Pallas kernels, on_device(): pl.pallas_call(kernel, out_shape=(jax.ShapeDtypeStruct((DB, DB), f32), ja...  105 us
    unnamed x5, local copies, waits for them, and re-layouts  2.98 us

profile of v4, /device:TPU:1, one launch (start us, length us, event | category | flops | bytes accessed | tf_op | source)
XLA Modules:
  0.0 110.9 jit_solution(17660991844223888618)
XLA Ops:
  0.6 1.4 %copy.9.grads = bf16[512,688]{1,0:T(8,128)(2,1)S(1)} copy(bf16[512,688]{0,1:T(8,128)(2,1)} %param.6) | data formatting | bytes 1409024 | tf_op args[1]
  2.0 0.0 copy-start
  2.0 0.9 copy-done
  3.0 0.0 copy-start.1
  3.0 0.7 copy-done.1
  3.6 105.4 %kfac.1 = (f32[256,256]{1,0:T(8,128)S(1)}, f32[688,688]{1,0:T(8,128)S(1)}, f32[688,256]{1,0:T(8,128)S(1)}, f32[688,256]{1,0:T(8,128)S(1)}) custom-call(bf16[512,4096]{1,0:T(8,128)(2,1)} %inp.1, bf16[512,688]{1,0:T(8,128)(2,1)S(1)} %copy.9.grads, s32[6]{0:T(128)S(1)} %copy-done.1, f32[256,256]{1,0:T(8,128)S(1)} %copy-done, f32[688,688]{1,0:T(8,128)} %g_inv.1), custom_call_target="tpu_custom_call" | custom-call | tf_op jit(solution)/shard_map/kfac/pallas_call | solution.py:441
  109.0 1.9 %store.1 = (f32[256,256]{1,0:T(8,128)}, f32[688,688]{1,0:T(8,128)}, f32[688,256]{1,0:T(8,128)}, f32[688,256]{1,0:T(8,128)}) custom-call(f32[256,256]{1,0:T(8,128)S(1)} %get-tuple-element.12.refs_0_, f32[688,688]{1,0:T(8,128)S(1)} %get-tuple-element.13.refs_1_, f32[688,256]{1,0:T(8,128)S(1)} %get-tuple-element.14.refs_2_, ...), custom_call_target="tpu_custom_call" | custom-call | tf_op jit(solution)/shard_map/store/pallas_call | solution.py:483
Async XLA Ops:
  2.0 1.0 copy-start
  3.0 0.7 copy-start.1

commit v5 on v3

--- a/solution.py
+++ b/solution.py
@@ -45,8 +45,8 @@
 
 
 def kernel(
-    inp, grads, use, a_inv, g_inv, a_out, g_out, w_out, p_out,
-    rg0, rg1, rx, mg, mx, fg, fx, sg, sx, acc_a, acc_g, acc_w, acc_p, ai, gi, ss, rs, ls,
+    inp, grads, use, a_out, g_out, w_out,
+    rg0, rg1, rx, mg, mx, fg, fx, sg, sx, acc_a, acc_g, acc_w, ss, rs, ls,
 ):
     s, t = lax.axis_index("section"), lax.axis_index("tensor")
     x, z = s // 4, s % 4
@@ -75,10 +75,6 @@
     def _():
         pl.semaphore_signal(bar, inc=1, device_id=(s, back), device_id_type=MESH)
 
-    loads = [
-        pltpu.make_async_copy(a_inv, ai, ls.at[0]),
-        pltpu.make_async_copy(g_inv, gi, ls.at[1]),
-    ]
 
     def share(ch, p):
         if ch == X:
@@ -90,7 +86,7 @@
         return (rg0, rx, rg1)[ch].at[k]
 
     own = [pltpu.make_async_copy(share(ch, s), slot(ch, N - 1), ls.at[2 + ch]) for ch in range(3)]
-    for cp in loads + own:
+    for cp in own:
         cp.start()
     pl.semaphore_wait(bar, 19 + (swap != t).astype(jnp.int32))
 
@@ -396,12 +392,6 @@
     w_step(1, 2)
     outs = [pltpu.make_async_copy(acc_w, w_out, ls.at[5])]
     outs[-1].start()
-    for cp in loads:
-        cp.wait()
-    left = exact(acc_w[...], ai[...], 1, 1)
-    acc_p[...] = exact(gi[...], left, 0, 0)
-    outs.append(pltpu.make_async_copy(acc_p, p_out, ls.at[7]))
-    outs[-1].start()
     c_in(GB)
     g_half(1)
     outs.append(pltpu.make_async_copy(acc_g, g_out, ls.at[6]))
@@ -421,13 +411,16 @@
     assert len(ids) <= 256, len(ids)
 
 
-def store(*refs):
-    sources, results, sems = refs[:4], refs[4:8], refs[8]
+def store(a_cov, g_cov, grad, a_inv, g_inv, a_out, g_out, w_out, p_out, prod, sems):
     copies = [
-        pltpu.make_async_copy(a, b, sems.at[i]) for i, (a, b) in enumerate(zip(sources, results))
+        pltpu.make_async_copy(p, q, sems.at[i])
+        for i, (p, q) in enumerate(((g_cov, g_out), (grad, w_out), (a_cov, a_out)))
     ]
     for cp in copies:
         cp.start()
+    prod[...] = exact(g_inv[...], exact(grad[...], a_inv[...], 1, 1), 0, 0)
+    copies.append(pltpu.make_async_copy(prod, p_out, sems.at[3]))
+    copies[-1].start()
     for cp in copies:
         cp.wait()
 
@@ -435,22 +428,19 @@
 def on_device(inputs, out_grads, use_section, a_inverse, g_inverse):
     bf, f32 = jnp.bfloat16, jnp.float32
     hbm = pl.BlockSpec(memory_space=pltpu.HBM)
-    a_cov, g_cov, grad, precond = pl.pallas_call(
+    a_cov, g_cov, grad = pl.pallas_call(
         kernel,
         out_shape=(
             jax.ShapeDtypeStruct((DB, DB), f32),
             jax.ShapeDtypeStruct((FB, FB), f32),
-            jax.ShapeDtypeStruct((FB, DB), f32),
             jax.ShapeDtypeStruct((FB, DB), f32),
         ),
         in_specs=[
             hbm,
             hbm,
             pl.BlockSpec(memory_space=pltpu.SMEM),
-            hbm,
-            hbm,
         ],
-        out_specs=(hbm,) * 4,
+        out_specs=(hbm,) * 3,
         scratch_shapes=[
             pltpu.VMEM((N, SUB, FB), bf),
             pltpu.VMEM((N, SUB, FB), bf),
@@ -464,9 +454,6 @@
             pltpu.VMEM((DB, DB), f32),
             pltpu.VMEM((FB, FB), f32),
             pltpu.VMEM((FB, DB), f32),
-            pltpu.VMEM((FB, DB), f32),
-            pltpu.VMEM((DB, DB), f32),
-            pltpu.VMEM((FB, FB), f32),
             pltpu.SemaphoreType.DMA((256,)),
             pltpu.SemaphoreType.DMA((256,)),
             pltpu.SemaphoreType.DMA((9,)),
@@ -475,17 +462,20 @@
             collective_id=0, has_side_effects=True, vmem_limit_bytes=48 * 2**20
         ),
         name="kfac",
-    )(inputs, out_grads, use_section, a_inverse, g_inverse)
-    results = (a_cov, g_cov, grad, precond)
+    )(inputs, out_grads, use_section)
+    vmem = pl.BlockSpec(memory_space=pltpu.VMEM)
+    whole = pl.BlockSpec(memory_space=pl.ANY)
     a_cov, g_cov, grad, precond = pl.pallas_call(
         store,
-        out_shape=tuple(jax.ShapeDtypeStruct(v.shape, f32) for v in results),
-        in_specs=[pl.BlockSpec(memory_space=pl.ANY)] * 4,
-        out_specs=(pl.BlockSpec(memory_space=pl.ANY),) * 4,
-        scratch_shapes=[pltpu.SemaphoreType.DMA((4,))],
-        compiler_params=pltpu.CompilerParams(vmem_limit_bytes=2**20),
+        out_shape=tuple(
+            jax.ShapeDtypeStruct(dims, f32) for dims in ((DB, DB), (FB, FB), (FB, DB), (FB, DB))
+        ),
+        in_specs=[whole, whole, vmem, vmem, vmem],
+        out_specs=(whole,) * 4,
+        scratch_shapes=[pltpu.VMEM((FB, DB), f32), pltpu.SemaphoreType.DMA((4,))],
+        compiler_params=pltpu.CompilerParams(vmem_limit_bytes=24 * 2**20),
         name="store",
-    )(*results)
+    )(a_cov, g_cov, grad, a_inverse, g_inverse)
     return a_cov, g_cov, grad.T, precond.T
 
 

time: 111 us -> 109 us (0.982)
  Pallas kernels: 108 us -> 106 us
    pallas_call x1, Pallas kernels: 106 us -> 103 us  [on_device(): pl.pallas_call(kernel, out_shape=(jax.ShapeDtypeStruct((DB, DB), f32), ja...]
    unnamed x5 -> x7, local copies, waits for them, and re-layouts: 2.98 us -> 2.03 us
where the time goes in v5:
time: 109 us
  Pallas kernels  106 us (97%)
  local copies, waits for them, and re-layouts  2.03 us (2%)
    pallas_call x1, Pallas kernels, on_device(): pl.pallas_call(kernel, out_shape=(jax.ShapeDtypeStruct((DB, DB), f32), ja...  103 us
    pallas_call x1, Pallas kernels, on_device(): pl.pallas_call(store, out_shape=tuple((jax.ShapeDtypeStruct(dims, f32) fo...  2.91 us

profile of v5, /device:TPU:1, one launch (start us, length us, event | category | flops | bytes accessed | tf_op | source)
XLA Modules:
  0.0 108.7 jit_solution(15460369673162498301)
XLA Ops:
  0.6 1.4 %copy.9.grads = bf16[512,688]{1,0:T(8,128)(2,1)S(1)} copy(bf16[512,688]{0,1:T(8,128)(2,1)} %param.6) | data formatting | bytes 1409024 | tf_op args[1]
  2.0 0.0 copy-start.2
  2.0 0.6 copy-done.2
  2.7 0.0 copy-start
  2.7 0.0 copy-start.1
  2.7 103.1 %kfac.1 = (f32[256,256]{1,0:T(8,128)S(1)}, f32[688,688]{1,0:T(8,128)S(1)}, f32[688,256]{1,0:T(8,128)S(1)}) custom-call(bf16[512,4096]{1,0:T(8,128)(2,1)} %inp.1, bf16[512,688]{1,0:T(8,128)(2,1)S(1)} %copy.9.grads, s32[6]{0:T(128)S(1)} %copy-done.2), custom_call_target="tpu_custom_call" | custom-call | tf_op jit(solution)/shard_map/kfac/pallas_call | solution.py:431
  105.8 0.0 copy-done
  105.8 0.0 copy-done.1
  105.8 2.9 %store.1 = (f32[256,256]{1,0:T(8,128)}, f32[688,688]{1,0:T(8,128)}, f32[688,256]{1,0:T(8,128)}, f32[688,256]{1,0:T(8,128)}) custom-call(f32[256,256]{1,0:T(8,128)S(1)} %get-tuple-element.11.a_cov, f32[688,688]{1,0:T(8,128)S(1)} %get-tuple-element.12.g_cov, f32[688,256]{1,0:T(8,128)S(1)} %get-tuple-element.13.grad, f32[256,256]{1,0:T(8,128)S(1)} %copy-done.1, ...), custom_call_target="tpu_custom_call" | custom-call | tf_op jit(solution)/shard_map/store/pallas_call | solution.py:468
Async XLA Ops:
  2.0 0.7 copy-start.2
  2.7 103.1 %copy-start = (f32[688,688]{1,0:T(8,128)S(1)}, f32[688,688]{1,0:T(8,128)}, u32[]{:S(2)}) copy-start(f32[688,688]{1,0:T(8,128)} %g_inv.1) | copy-start | bytes 5680132
  2.7 103.1 %copy-start.1 = (f32[256,256]{1,0:T(8,128)S(1)}, f32[256,256]{1,0:T(8,128)}, u32[]{:S(2)}) copy-start(f32[256,256]{1,0:T(8,128)} %a_inv.1) | copy-start | bytes 786436
